TPU v7x, 32 devices: a whole 2x2x4 slice. The times are simulated.
32 devices in a mesh: groups: 2 (over x), rows: 16 (over z, y, core).
Axes of the slice: x: 2, y: 2, z: 4, core: 2. Of those that a mesh axis runs over, the one named last changes fastest.
Arguments:
- planes: bfloat16 [6, 48, 48, 256], P('groups', 'rows'), parts along dimension 0, may hold values from -6 to 6
- conv_weight: bfloat16 [3, 3, 3, 256, 256], P(None, None, None, 'rows'), may hold values from -0.125 to 0.125
Outputs:
- mixed: bfloat16 [6, 48, 48, 256], P('groups', 'rows'), parts along dimension 0
There are 2 independent parts, one for each index of `groups`. A program takes and returns all parts, laid end to end along the dimension named above; an argument that names none is the same for every part. Nothing has to cross between parts.
All inputs are finite; a program needn't handle non-finite values.
Results may differ from a plain program's by a relative error of at most 0.0034.
Values may be sent and summed in bfloat16 or wider, within the bound.
A program may use at most 128 MiB of HBM per device.

v0:
```python
import jax
import jax.numpy as jnp
from jax import lax
from jax.sharding import PartitionSpec as P


def extended(block, sides, width):
    for axis, dim in sides:
        count = lax.axis_size(axis)
        forward = [(i, i + 1) for i in range(count - 1)]
        backward = [(target, source) for source, target in forward]
        low = lax.ppermute(
            lax.slice_in_dim(block, block.shape[dim] - width, None, axis=dim), axis, forward
        )
        high = lax.ppermute(lax.slice_in_dim(block, 0, width, axis=dim), axis, backward)
        block = jnp.concatenate([low, block, high], axis=dim)
    return block


def conv_block(padded, band, width, chans, piece):
    count = piece.shape[3]
    windows = []
    for block in range(3):
        sliced = lax.dynamic_slice_in_dim(padded, block * chans, count, 3)
        for krow in range(3):
            for kcol in range(3):
                windows.append(sliced[:, krow : krow + band, kcol : kcol + width, :])
    columns = jnp.concatenate(windows, axis=3)
    flat = piece.reshape(27 * count, chans)
    return jnp.einsum("prjc,cd->prjd", columns, flat, preferred_element_type=jnp.float32)


def body(planes, conv_weight):
    band = planes.shape[1]
    width = planes.shape[2]
    chans = planes.shape[3]
    row_sums = jnp.sum(planes, axis=2, dtype=jnp.float32)
    col_parts = jnp.sum(planes, axis=1, dtype=jnp.float32)
    line_u0 = (row_sums[1] / width).astype(jnp.bfloat16)
    line_u1 = (row_sums[0] / width).astype(jnp.bfloat16)
    means_yz = (row_sums[2] / width).astype(jnp.bfloat16)
    position = lax.axis_index("rows") * band
    totals = lax.psum((col_parts[0], col_parts[1], col_parts[2]), "rows")
    full_u2 = (totals[0] / width).astype(jnp.bfloat16)
    line_v1 = (totals[2] / width).astype(jnp.bfloat16)
    line_v2 = (totals[1] / width).astype(jnp.bfloat16)
    line_v0 = lax.all_gather(means_yz, "rows", axis=0, tiled=True)
    line_u2 = lax.dynamic_slice_in_dim(full_u2, position, band, 0)
    col_lines = jnp.stack([line_v0, line_v1, line_v2], axis=0)
    shape = planes.shape
    row_lines = jnp.stack([line_u0, line_u1, line_u2], axis=0)
    upper = jnp.broadcast_to(row_lines[:, :, None, :], shape)
    lower = jnp.broadcast_to(col_lines[:, None, :, :], shape)
    stacked = jnp.concatenate([planes, upper, lower], axis=3)
    padded = extended(stacked, (("rows", 1),), 1)
    padded = jnp.pad(padded, ((0, 0), (0, 0), (1, 1), (0, 0)))
    summed = conv_block(
        padded, band, width, chans, lax.all_gather(conv_weight, "rows", axis=3, tiled=True)
    )
    return summed.astype(jnp.bfloat16)


def solution(mesh):
    placed = (P("groups", "rows", None, None), P(None, None, None, "rows", None))
    return jax.shard_map(
        body, mesh=mesh, in_specs=placed, out_specs=P("groups", "rows", None, None), check_vma=False
    )
```

profile of v0, /device:TPU:0, one launch (start us, length us, event | category | flops | bytes accessed | tf_op | source)
XLA Modules:
  0.0 169.9 jit_solution(5290120772060771789)
XLA Ops:
  6.5 0.0 copy-start
  6.5 0.0 all-reduce.4.cloned.1.call-start
  6.5 1.1 convert_reduce_fusion.1
  7.6 0.7 slice_bitcast_fusion.2
  8.3 0.0 all-reduce.4.cloned.1.call-update
  8.3 0.0 all-gather.3.cloned.1.call-start
  8.3 0.7 all-gather.3.cloned.1.call-update
  9.1 23.2 %all-gather = bf16[1,48,256]{2,0,1:T(2,128)(2,1)S(1)} all-gather(bf16[1,3,256]{2,0,1:T(2,128)(2,1)S(1)} %copy.6), channel_id=2, replica_groups=mesh['groups'=2,'rows'=16] {'rows'}, dimensions={1}, use_global_device_ids=true | all-gather | bytes 26112 | tf_op jit(solution)/shard_map/all_gather | solution.py:47
  32.3 70.0 %all-reduce.4.cloned.1.call-done = (f32[48,256]{1,0:T(8,128)}, f32[48,256]{1,0:T(8,128)}, f32[48,256]{1,0:T(8,128)}) async-done(((f32[48,256]{1,0:T(8,128)}, f32[48,256]{1,0:T(8,128)}, f32[48,256]{1,0:T(8,128)}), (f32[48,256]{1,0:T(8,128)}, f32[48,256]{1,0:T(8,128)}, f32[48,256]{1,0:T(8,128)})) %all-reduce.4.cloned.1.call-update) | async-done | bytes 147472 | tf_op jit(solution)/shard_map/psum | solution.py:43
  102.3 0.7 fusion.14
  103.0 0.8 fusion.8
  103.9 1.0 pad_maximum_fusion.8
  104.9 1.3 collective-permute-start
  106.2 1.3 collective-permute-start.1
  107.5 0.0 collective-permute-done
  107.5 3.2 %collective-permute-done.1 = bf16[3,1,48,768]{3,2,1,0:T(8,128)(2,1)S(1)} collective-permute-done((bf16[3,1,48,768]{3,2,1,0:T(8,128)(2,1)S(1)}, bf16[3,1,48,768]{3,2,1,0:T(8,128)(2,1)S(1)}, u32[]{:S(2)}, u32[]{:S(2)}) %collective-permute-start.1) | collective-permute-done | bytes 221216 | tf_op jit(solution)/shard_map/ppermute | solution.py:15
  110.7 1.4 select_maximum_fusion
  112.1 0.7 slice_dynamic-update-slice_fusion.17
  112.8 0.0 copy-done
  112.8 0.8 maximum_dynamic-update-slice_fusion.3
  113.6 0.8 slice_dynamic-update-slice_fusion.16
  114.3 0.8 slice_dynamic-update-slice_fusion.15
  115.1 0.7 constant_dynamic-update-slice_fusion
  115.8 0.8 slice_dynamic-update-slice_fusion.14
  116.6 0.8 slice_dynamic-update-slice_fusion.13
  117.4 0.7 maximum_dynamic-update-slice_fusion.2
  118.1 0.8 slice_dynamic-update-slice_fusion.12
  118.9 0.7 slice_dynamic-update-slice_fusion.11
  119.6 0.7 maximum_dynamic-update-slice_fusion.1
  120.3 0.8 slice_dynamic-update-slice_fusion.10
  121.1 0.7 slice_dynamic-update-slice_fusion.9
  121.8 0.7 broadcast_dynamic-update-slice_fusion.1
  122.5 0.8 slice_dynamic-update-slice_fusion.8
  123.3 0.7 slice_dynamic-update-slice_fusion.7
  124.0 0.8 maximum_dynamic-update-slice_fusion
  124.8 0.8 slice_dynamic-update-slice_fusion.6
  125.6 0.7 slice_dynamic-update-slice_fusion.5
  126.3 0.7 fusion.7
  127.0 0.8 slice_dynamic-update-slice_fusion.4
  127.8 0.7 slice_dynamic-update-slice_fusion.3
  128.5 0.7 broadcast_dynamic-update-slice_fusion
  129.2 0.8 slice_dynamic-update-slice_fusion.2
  130.1 0.7 slice_dynamic-update-slice_fusion.1
  130.8 0.7 fusion.6
  131.5 0.8 slice_dynamic-update-slice_fusion
  132.3 24.6 %all-gather.3.cloned.1.call-done = bf16[3,3,3,256,256]{4,3,2,1,0:T(8,128)(2,1)} async-done(((bf16[3,3,3,16,256]{4,3,2,1,0:T(8,128)(2,1)}), bf16[3,3,3,256,256]{4,3,2,1,0:T(8,128)(2,1)}) %all-gather.3.cloned.1.call-update) | async-done | bytes 3538960 | tf_op jit(solution)/shard_map/all_gather | solution.py:58
  156.9 6.1 %convolution_convert_fusion = bf16[3,3,48,256]{3,2,1,0:T(8,128)(2,1)} fusion(bf16[3,3,48,6912]{3,2,1,0:T(8,128)(2,1)} %slice_dynamic-update-slice_fusion, bf16[6912,256,1,1]{1,0,3,2:T(8,128)(2,1)} %bitcast.19), kind=kOutput, calls=%fused_computation.10 | convolution fusion | flops 1528934400 | bytes 9732096 | tf_op jit(solution)/shard_map/prjc,cd->prjd/dot_general | solution.py:30
  (7 shorter events, 0.1 us)
Async XLA Ops:
  6.5 106.3 %copy-start = (bf16[3,3,48,256]{3,2,1,0:T(8,128)(2,1)S(1)}, bf16[3,3,48,256]{3,2,1,0:T(8,128)(2,1)}, u32[]{:S(2)}) copy-start(bf16[3,3,48,256]{3,2,1,0:T(8,128)(2,1)} %param.2) | copy-start | bytes 663556
  6.5 95.8 %all-reduce.4.cloned.1.call-start = ((), (), s32[]{:S(2)}) async-start(), calls=%async_computation.1 | async-start | bytes 294912 | tf_op jit(solution)/shard_map/psum | solution.py:43
  8.3 148.6 %all-gather.3.cloned.1.call-start = ((), (), s32[]{:S(2)}) async-start(), calls=%async_computation | async-start | bytes 3760128 | tf_op jit(solution)/shard_map/all_gather | solution.py:58
  104.9 2.6 %collective-permute-start = (bf16[3,1,48,768]{3,2,1,0:T(8,128)(2,1)S(1)}, bf16[3,1,48,768]{3,2,1,0:T(8,128)(2,1)S(1)}, u32[]{:S(2)}, u32[]{:S(2)}) collective-permute-start(bf16[3,1,48,768]{3,2,1,0:T(8,128)(2,1)S(1)} %get-tuple-element.10), channel_id=1, source_target_pairs={{0,1},{1,2},{2,3},{3,4},{4,5},{5,6},{6,7},{7,8},{8,9},{9,10},{10,1... | collective-permute-start | bytes 663560 | tf_op jit(solution)/shard_map/ppermute | solution.py:12
  106.2 4.5 %collective-permute-start.1 = (bf16[3,1,48,768]{3,2,1,0:T(8,128)(2,1)S(1)}, bf16[3,1,48,768]{3,2,1,0:T(8,128)(2,1)S(1)}, u32[]{:S(2)}, u32[]{:S(2)}) collective-permute-start(bf16[3,1,48,768]{3,2,1,0:T(8,128)(2,1)S(1)} %get-tuple-element.11), channel_id=1, source_target_pairs={{1,0},{2,1},{3,2},{4,3},{5,4},{6,5},{7,6},{8,7},{9,8},{10,9},{11,1... | collective-permute-start | bytes 663560 | tf_op jit(solution)/shard_map/ppermute | solution.py:15
Sparse Core Ops, SparseCore 0:
  11.1 91.1 all-reduce.3
  104.5 52.4 all-gather.2
where the time goes:
time: 170 us
  waiting for transfers between devices  98.5 us (58%)
  blocking collectives  23.2 us (14%)
  local copies, waits for them, and re-layouts  16.5 us (10%)
  between operations  13.5 us (8%)
  other arithmetic  9.42 us (6%)
  matrix products  6.14 us (4%)
  starting transfers between devices  2.64 us (2%)
    psum x1, waiting for transfers between devices, body(): totals = lax.psum((col_parts[0], col_parts[1], col_parts[2]), 'rows')  70 us
    all_gather x1, waiting for transfers between devices, body(): lax.all_gather(conv_weight, 'rows', axis=3, tiled=True)  24.6 us
    all_gather x1, blocking collectives, body(): line_v0 = lax.all_gather(means_yz, 'rows', axis=0, tiled=True)  23.2 us
    unnamed x22, local copies, waits for them, and re-layouts  15 us
    dot_general x1, matrix products, conv_block(): jnp.einsum('prjc,cd->prjd', columns, flat, preferred_element_type=jnp.flo...  6.14 us
    unnamed x6, other arithmetic  4.43 us
  transfers between devices with their start and end apart: 4, of which 3 were waited for; matrix products, arithmetic and copies ran while one was open for 14% of the time, Pallas kernels for 0%

commit v1 on v0

--- a/solution.py
+++ b/solution.py
@@ -1,7 +1,293 @@
+import functools
+
 import jax
 import jax.numpy as jnp
 from jax import lax
+from jax.experimental import pallas as pl
+from jax.experimental.pallas import tpu as pltpu
 from jax.sharding import PartitionSpec as P
+
+MESH = pl.DeviceIdType.MESH
+PAD = 16
+
+
+def fused(n, split, planes, w, out, wbuf, xpad, cown, crecv, lsend, lines, vbuf, ubuf, ybuf,
+          wsend, wrecv, hsend, hrecv, csem, crsem, lsem, lrsem):
+    band, width, chans = planes.shape[1:]
+    count = w.shape[1]
+    nz = n // 4
+    g = lax.axis_index("groups")
+    me = lax.axis_index("rows")
+    z, y, core = me // 4, (me // 2) % 2, me % 2
+
+    def rank(zz, yy, cc):
+        return (zz * 2 + yy) * 2 + cc
+
+    partner = (g, rank(z, y, 1 - core))
+    across = (g, rank(z, 1 - y, core))
+    above = (g, lax.rem(me + 4, n))
+    below = (g, lax.rem(me + n - 4, n))
+    twin = (1 - g, me)
+
+    barrier = pltpu.get_barrier_semaphore()
+    for off in range(1, n):
+        pl.semaphore_signal(barrier, inc=1, device_id=(g, lax.rem(me + off, n)), device_id_type=MESH)
+    if split:
+        pl.semaphore_signal(barrier, inc=1, device_id=twin, device_id_type=MESH)
+
+    wbuf[:, pl.ds(pl.multiple_of(me * count, count), count), :] = w[...]
+    xpad[:, 1:band + 1] = planes[...]
+
+    @pl.when(me == 0)
+    def _():
+        xpad[:, 0] = jnp.zeros((3, width, chans), xpad.dtype)
+
+    @pl.when(me == n - 1)
+    def _():
+        xpad[:, band + 1] = jnp.zeros((3, width, chans), xpad.dtype)
+
+    pl.semaphore_wait(barrier, n if split else n - 1)
+
+    sends = []
+
+    def start(cond, k, s, dev):
+        region = wbuf.at[pl.ds(9 * k, 9), pl.ds(pl.multiple_of(s * count, count), count), :]
+        copy = pltpu.make_async_remote_copy(
+            src_ref=region, dst_ref=region, send_sem=wsend.at[len(sends)], recv_sem=wrecv.at[k, s],
+            device_id=dev, device_id_type=MESH)
+        pl.when(cond)(copy.start)
+        sends.append((cond, copy))
+
+    def landed(k, s):
+        region = wbuf.at[pl.ds(9 * k, 9), pl.ds(pl.multiple_of(s * count, count), count), :]
+        pltpu.make_async_remote_copy(
+            src_ref=region, dst_ref=region, send_sem=wsend.at[0], recv_sem=wrecv.at[k, s],
+            device_id=partner, device_id_type=MESH).wait_recv()
+
+    always = me >= 0
+
+    def mine(zz):
+        return lax.rem(zz + g, 2) == 0 if split else zz >= 0
+
+    def along(k, zz, up, down, valid):
+        s = rank(zz, y, core)
+        if up:
+            start(valid & (z < nz - 1), k, s, above)
+        if down:
+            start(valid & (z > 0), k, s, below)
+        start(valid & mine(zz), k, s, across)
+        start(valid, k, s, partner)
+
+    def sideways(k, zz, valid):
+        s = rank(zz, 1 - y, core)
+
+        @pl.when(valid & mine(zz))
+        def _():
+            landed(k, s)
+        if split:
+            start(valid & mine(zz), k, s, twin)
+        start(valid & mine(zz), k, s, partner)
+
+    def third(k, zz, valid):
+        s = rank(zz, 1 - y, core)
+        cond = valid & jnp.logical_not(mine(zz))
+
+        @pl.when(cond)
+        def _():
+            landed(k, s)
+        start(cond, k, s, partner)
+
+    for k in range(3):
+        along(k, z, True, True, always)
+
+    low = pltpu.make_async_remote_copy(
+        src_ref=planes.at[:, band - 1], dst_ref=xpad.at[:, 0], send_sem=hsend.at[0], recv_sem=hrecv.at[0],
+        device_id=(g, lax.rem(me + 1, n)), device_id_type=MESH)
+    high = pltpu.make_async_remote_copy(
+        src_ref=planes.at[:, 0], dst_ref=xpad.at[:, band + 1], send_sem=hsend.at[1], recv_sem=hrecv.at[1],
+        device_id=(g, lax.rem(me + n - 1, n)), device_id_type=MESH)
+    pl.when(me < n - 1)(low.start)
+    pl.when(me > 0)(high.start)
+
+    for p in range(3):
+        total = planes[p, 0].astype(jnp.float32)
+        for i in range(1, band):
+            total = total + planes[p, i].astype(jnp.float32)
+        for d in range(n):
+            cown[d, p * band:(p + 1) * band, :] = total[d * band:(d + 1) * band, :]
+    ccopies = []
+    for off in range(1, n):
+        peer = lax.rem(me + off, n)
+        copy = pltpu.make_async_remote_copy(
+            src_ref=cown.at[peer], dst_ref=crecv.at[off - 1], send_sem=csem.at[off - 1],
+            recv_sem=crsem.at[off - 1], device_id=(g, peer), device_id_type=MESH)
+        copy.start()
+        ccopies.append(copy)
+    lsend[...] = jnp.zeros(lsend.shape, lsend.dtype)
+    rows = []
+    for p in range(3):
+        for i in range(band):
+            rows.append(jnp.sum(planes[p, i].astype(jnp.float32), axis=0, keepdims=True) / width)
+    for index, row in enumerate(rows):
+        lsend[PAD + index:PAD + index + 1, :] = row
+
+    def step(d):
+        for k in range(3):
+            for zz, up, down, valid in ((z - d, True, False, z - d >= 0), (z + d, False, True, z + d < nz)):
+                s = rank(zz, y, core)
+
+                @pl.when(valid)
+                def _():
+                    landed(k, s)
+                along(k, zz, up, down, valid)
+            for zz, valid in spread(d - 1):
+                sideways(k, zz, valid)
+            if split and d >= 2:
+                for zz, valid in spread(d - 2):
+                    third(k, zz, valid)
+
+    def spread(d):
+        if d == 0:
+            return [(z, always)]
+        return [(z - d, z - d >= 0), (z + d, z + d < nz)]
+
+    step(1)
+
+    for copy in ccopies:
+        copy.wait_recv()
+    total = cown[me][0:3 * band]
+    for off in range(1, n):
+        total = total + crecv[off - 1, 0:3 * band, :]
+    lsend[0:3 * band, :] = total / width
+    lines[me] = lsend[...].astype(jnp.bfloat16)
+    lcopies = []
+    for off in range(1, n):
+        peer = lax.rem(me + off, n)
+        copy = pltpu.make_async_remote_copy(
+            src_ref=lines.at[me], dst_ref=lines.at[me], send_sem=lsem.at[off - 1],
+            recv_sem=lrsem.at[me], device_id=(g, peer), device_id_type=MESH)
+        copy.start()
+        lcopies.append(copy)
+
+    for d in range(2, nz):
+        step(d)
+    for k in range(3):
+        for zz, valid in spread(nz - 1):
+            sideways(k, zz, valid)
+    if split:
+        for d in (nz - 2, nz - 1):
+            for k in range(3):
+                for zz, valid in spread(d):
+                    third(k, zz, valid)
+
+    @pl.when(me > 0)
+    def _():
+        low.wait_recv()
+
+    @pl.when(me < n - 1)
+    def _():
+        high.wait_recv()
+
+    def gathered(k):
+        for zz in range(nz):
+            for yy in range(2):
+                landed(k, rank(zz, yy, 1 - core))
+
+    gathered(0)
+    for b in range(3):
+        for p in range(3):
+            acc = None
+            for a in range(3):
+                lhs = xpad[p, a:a + band].reshape(band * width, chans)
+                part = jnp.dot(lhs, wbuf[a * 3 + b], preferred_element_type=jnp.float32)
+                acc = part if acc is None else acc + part
+            ybuf[b, p] = acc.reshape(band, width, chans)
+
+    for off in range(1, n):
+        src = lax.rem(me + off, n)
+        pltpu.make_async_remote_copy(
+            src_ref=lines.at[src], dst_ref=lines.at[src], send_sem=lsem.at[0], recv_sem=lrsem.at[src],
+            device_id=partner, device_id_type=MESH).wait_recv()
+    vrows = (PAD + 2 * band, 2 * band, band)
+    for s in range(n):
+        block = lines[s].astype(jnp.float32)
+        for p in range(3):
+            vbuf[p * width + s * band:p * width + (s + 1) * band, :] = block[vrows[p]:vrows[p] + band, :]
+    urows = (PAD + band, PAD, 0)
+    before = lines[jnp.maximum(me - 1, 0)].astype(jnp.float32)
+    here = lines[me].astype(jnp.float32)
+    after = lines[jnp.minimum(me + 1, n - 1)].astype(jnp.float32)
+    ubuf[...] = jnp.zeros(ubuf.shape, ubuf.dtype)
+    depth = ubuf.shape[0] // 3
+    for p in range(3):
+        at = urows[p]
+        ubuf[p * depth + 1:p * depth + 1 + band, :] = here[at:at + band, :]
+        first = before[at + band - 1:at + band, :]
+        last = after[at:at + 1, :]
+        ubuf[p * depth:p * depth + 1, :] = jnp.where(me > 0, first, jnp.zeros_like(first))
+        ubuf[p * depth + band + 1:p * depth + band + 2, :] = jnp.where(me < n - 1, last, jnp.zeros_like(last))
+
+    gathered(1)
+    gathered(2)
+    ulhs = ubuf[...].astype(jnp.bfloat16)
+    vlhs = vbuf[...].astype(jnp.bfloat16)
+    u_all, v_all = [], []
+    for b in range(3):
+        u_all.append([jnp.dot(ulhs, wbuf[9 + a * 3 + b], preferred_element_type=jnp.float32) for a in range(3)])
+    column = lax.broadcasted_iota(jnp.int32, (width, chans), 0)
+    for p in range(3):
+        vp = vlhs[p * width:(p + 1) * width]
+        v_all = [[jnp.dot(vp, wbuf[18 + a * 3 + b], preferred_element_type=jnp.float32) for a in range(3)]
+                 for b in range(3)]
+        for i in range(band):
+            terms = []
+            for b in range(3):
+                top, mid, bottom = v_all[b]
+                if i == 0:
+                    top = jnp.where(me > 0, top, jnp.zeros_like(top))
+                if i == band - 1:
+                    bottom = jnp.where(me < n - 1, bottom, jnp.zeros_like(bottom))
+                line = sum(u_all[b][a][p * depth + i + a:p * depth + i + a + 1, :] for a in range(3))
+                terms.append(ybuf[b, p, i] + (top + mid + bottom) + line)
+            left = jnp.where(column == 0, 0.0, pltpu.roll(terms[0], 1, 0))
+            right = jnp.where(column == width - 1, 0.0, pltpu.roll(terms[2], width - 1, 0))
+            out[p, i] = (left + terms[1] + right).astype(out.dtype)
+
+    for cond, copy in sends:
+        pl.when(cond)(copy.wait_send)
+    pl.when(me < n - 1)(low.wait_send)
+    pl.when(me > 0)(high.wait_send)
+    for copy in ccopies + lcopies:
+        copy.wait_send()
+
+
+def banded(n, split, planes, conv_weight):
+    band, width, chans = planes.shape[1:]
+    count = conv_weight.shape[3]
+    depth = -(-(band + 2) // 8) * 8
+    vmem = pl.BlockSpec(memory_space=pltpu.VMEM)
+    dma = pltpu.SemaphoreType.DMA
+    return pl.pallas_call(
+        functools.partial(fused, n, split),
+        out_shape=jax.ShapeDtypeStruct(planes.shape, planes.dtype),
+        in_specs=[vmem, vmem],
+        out_specs=vmem,
+        scratch_shapes=[
+            pltpu.VMEM((27, chans, chans), jnp.bfloat16),
+            pltpu.VMEM((3, band + 2, width, chans), jnp.bfloat16),
+            pltpu.VMEM((n, PAD, chans), jnp.float32),
+            pltpu.VMEM((n - 1, PAD, chans), jnp.float32),
+            pltpu.VMEM((2 * PAD, chans), jnp.float32),
+            pltpu.VMEM((n, 2 * PAD, chans), jnp.bfloat16),
+            pltpu.VMEM((3 * width, chans), jnp.float32),
+            pltpu.VMEM((3 * depth, chans), jnp.float32),
+            pltpu.VMEM((3, 3, band, width, chans), jnp.float32),
+            dma((160,)), dma((3, n)), dma((2,)), dma((2,)),
+            dma((n - 1,)), dma((n - 1,)), dma((n - 1,)), dma((n,)),
+        ],
+        compiler_params=pltpu.CompilerParams(
+            collective_id=0, has_side_effects=True, vmem_limit_bytes=40 * 1024 * 1024),
+    )(planes, conv_weight.reshape(27, count, chans))
 
 
 def extended(block, sides, width):
@@ -61,7 +347,17 @@
 
 
 def solution(mesh):
+    n = mesh.shape["rows"]
+    split = mesh.shape["groups"] == 2
+
+    def local(planes, conv_weight):
+        band, width, chans = planes.shape[1:]
+        fits = n % 4 == 0 and 3 * band <= PAD and width % 16 == 0 and conv_weight.shape[3] % 16 == 0
+        if fits and band * n == width:
+            return banded(n, split, planes, conv_weight)
+        return body(planes, conv_weight)
+
     placed = (P("groups", "rows", None, None), P(None, None, None, "rows", None))
     return jax.shard_map(
-        body, mesh=mesh, in_specs=placed, out_specs=P("groups", "rows", None, None), check_vma=False
+        local, mesh=mesh, in_specs=placed, out_specs=P("groups", "rows", None, None), check_vma=False
     )

time: 170 us -> 45.5 us (0.27)
  waiting for transfers between devices: 98.5 us -> 0 us
  Pallas kernels: 0 us -> 42.8 us
  blocking collectives: 23.2 us -> 0 us
  local copies, waits for them, and re-layouts: 16.5 us -> 2.56 us
  between operations: 13.5 us -> 0.01 us
  other arithmetic: 9.42 us -> 0 us
  matrix products: 6.14 us -> 0 us
  starting transfers between devices: 2.64 us -> 0 us
    psum x1 -> x0, waiting for transfers between devices: 70 us -> none  [body(): totals = lax.psum((col_parts[0], col_parts[1], col_parts[2]), 'rows')]
    pallas_call x0 -> x1, Pallas kernels: none -> 42.8 us  [banded(): pl.pallas_call(functools.partial(fused, n, split), out_shape=jax.ShapeDty...]
    all_gather x1 -> x0, waiting for transfers between devices: 24.6 us -> none  [body(): lax.all_gather(conv_weight, 'rows', axis=3, tiled=True)]
    all_gather x1 -> x0, blocking collectives: 23.2 us -> none  [body(): line_v0 = lax.all_gather(means_yz, 'rows', axis=0, tiled=True)]
    unnamed x22 -> x5, local copies, waits for them, and re-layouts: 15 us -> 2.56 us
    dot_general x1 -> x0, matrix products: 6.14 us -> none  [conv_block(): jnp.einsum('prjc,cd->prjd', columns, flat, preferred_element_type=jnp.flo...]
    unnamed x6 -> x0, other arithmetic: 4.43 us -> none
    ppermute x2 -> x0, waiting for transfers between devices: 3.17 us -> none  [the longest x1 3.17 us: extended(): lax.ppermute(lax.slice_in_dim(block, 0, width, axis=dim), axis, backward)]
  transfers between devices with their start and end apart: 4 -> 0, of which waited for: 3 -> 0; matrix products, arithmetic and copies ran while one was open for 14% -> 0% of each run, Pallas kernels for 0% -> 0%
where the time goes in v1:
time: 45.5 us; the launch traced here: 45.3 us
  Pallas kernels  42.8 us (94%)
  local copies, waits for them, and re-layouts  2.56 us (6%)
    pallas_call x1, Pallas kernels, banded(): pl.pallas_call(functools.partial(fused, n, split), out_shape=jax.ShapeDty...  42.8 us
    unnamed x5, local copies, waits for them, and re-layouts  2.56 us

profile of v1, /device:TPU:0, one launch (start us, length us, event | category | flops | bytes accessed | tf_op | source)
XLA Modules:
  0.0 45.3 jit_solution(2956018209711992015)
XLA Ops:
  0.0 0.0 copy-start
  0.0 0.9 %copy-done = bf16[3,3,48,256]{3,2,1,0:T(8,128)(2,1)S(1)} copy-done((bf16[3,3,48,256]{3,2,1,0:T(8,128)(2,1)S(1)}, bf16[3,3,48,256]{3,2,1,0:T(8,128)(2,1)}, u32[]{:S(2)}) %copy-start) | copy-done | bytes 221208
  0.9 0.0 copy-start.1
  0.9 0.9 %copy-done.1 = bf16[3,3,3,16,256]{4,3,2,1,0:T(8,128)(2,1)S(1)} copy-done((bf16[3,3,3,16,256]{4,3,2,1,0:T(8,128)(2,1)S(1)}, bf16[3,3,3,16,256]{4,3,2,1,0:T(8,128)(2,1)}, u32[]{:S(2)}) %copy-start.1) | copy-done | bytes 221208
  1.9 42.8 %shard_map.28 = bf16[3,3,48,256]{3,2,1,0:T(8,128)(2,1)S(1)} custom-call(bf16[3,3,48,256]{3,2,1,0:T(8,128)(2,1)S(1)} %copy-done, bf16[27,16,256]{2,1,0:T(8,128)(2,1)S(1)} %bitcast.1), custom_call_target="tpu_custom_call" | custom-call | tf_op jit(solution)/shard_map/pallas_call | solution.py:270
  44.7 0.7 %copy.4 = bf16[3,3,48,256]{3,2,1,0:T(8,128)(2,1)} copy(bf16[3,3,48,256]{3,2,1,0:T(8,128)(2,1)S(1)} %shard_map.28) | data formatting | bytes 442368
Async XLA Ops:
  0.0 0.9 %copy-start = (bf16[3,3,48,256]{3,2,1,0:T(8,128)(2,1)S(1)}, bf16[3,3,48,256]{3,2,1,0:T(8,128)(2,1)}, u32[]{:S(2)}) copy-start(bf16[3,3,48,256]{3,2,1,0:T(8,128)(2,1)} %planes.1) | copy-start | bytes 663556
  0.9 0.9 %copy-start.1 = (bf16[3,3,3,16,256]{4,3,2,1,0:T(8,128)(2,1)S(1)}, bf16[3,3,3,16,256]{4,3,2,1,0:T(8,128)(2,1)}, u32[]{:S(2)}) copy-start(bf16[3,3,3,16,256]{4,3,2,1,0:T(8,128)(2,1)} %param.3) | copy-start | bytes 663556

commit v2 on v1

--- a/solution.py
+++ b/solution.py
@@ -11,9 +11,10 @@
 PAD = 16
 
 
-def fused(n, split, planes, w, out, wbuf, xpad, cown, crecv, lsend, lines, vbuf, ubuf, ybuf,
-          wsend, wrecv, hsend, hrecv, csem, crsem, lsem, lrsem):
+def fused(n, split, planes, w, out, wbuf, xpad, cown, cpart, crecv, lsend, lines, vbuf, ubuf, ybuf,
+          wsend, wrecv, hsend, hrecv, psem, csem, crsem, lsem, lrsem, fsem, local):
     band, width, chans = planes.shape[1:]
+    half = n // 2
     count = w.shape[1]
     nz = n // 4
     g = lax.axis_index("groups")
@@ -29,14 +30,20 @@
     below = (g, lax.rem(me + n - 4, n))
     twin = (1 - g, me)
 
+    own_planes = pltpu.make_async_copy(planes, xpad.at[:, pl.ds(1, band)], local.at[0])
+    own_planes.start()
+    own_weights = pltpu.make_async_copy(
+        w, wbuf.at[:, pl.ds(pl.multiple_of(me * count, count), count), :], local.at[1])
+    own_weights.start()
+
+    def peer(off):
+        return (g, lax.rem(me + 2 * off, n))
+
     barrier = pltpu.get_barrier_semaphore()
-    for off in range(1, n):
-        pl.semaphore_signal(barrier, inc=1, device_id=(g, lax.rem(me + off, n)), device_id_type=MESH)
-    if split:
-        pl.semaphore_signal(barrier, inc=1, device_id=twin, device_id_type=MESH)
-
-    wbuf[:, pl.ds(pl.multiple_of(me * count, count), count), :] = w[...]
-    xpad[:, 1:band + 1] = planes[...]
+    greeted = [peer(off) for off in range(1, half)]
+    greeted += [partner, (g, lax.rem(me + n - 1 + 2 * core, n))] + ([twin] if split else [])
+    for device in greeted:
+        pl.semaphore_signal(barrier, inc=1, device_id=device, device_id_type=MESH)
 
     @pl.when(me == 0)
     def _():
@@ -46,7 +53,20 @@
     def _():
         xpad[:, band + 1] = jnp.zeros((3, width, chans), xpad.dtype)
 
-    pl.semaphore_wait(barrier, n if split else n - 1)
+    own_planes.wait()
+    for p in range(3):
+        total = xpad[p, 1].astype(jnp.float32)
+        for i in range(1, band):
+            total = total + xpad[p, 1 + i].astype(jnp.float32)
+        for d in range(n):
+            cown[d % 2, d // 2, p * band:(p + 1) * band, :] = total[d * band:(d + 1) * band, :]
+    pl.semaphore_wait(barrier, len(greeted))
+
+    swap = pltpu.make_async_remote_copy(
+        src_ref=cown.at[1 - core], dst_ref=cpart, send_sem=psem.at[0], recv_sem=psem.at[1],
+        device_id=partner, device_id_type=MESH)
+    swap.start()
+    own_weights.wait()
 
     sends = []
 
@@ -69,12 +89,13 @@
     def mine(zz):
         return lax.rem(zz + g, 2) == 0 if split else zz >= 0
 
-    def along(k, zz, up, down, valid):
+    def along(k, zz, up, down, valid, last=False):
         s = rank(zz, y, core)
+        first = lax.rem(core + g, 2) == 0 if split else always
         if up:
-            start(valid & (z < nz - 1), k, s, above)
+            start(valid & (z < nz - 1) & (first if last else always), k, s, above)
         if down:
-            start(valid & (z > 0), k, s, below)
+            start(valid & (z > 0) & (first if last else always), k, s, below)
         start(valid & mine(zz), k, s, across)
         start(valid, k, s, partner)
 
@@ -97,39 +118,35 @@
             landed(k, s)
         start(cond, k, s, partner)
 
-    for k in range(3):
-        along(k, z, True, True, always)
+    along(0, z, True, True, always)
+    swap.wait_recv()
+    ccopies = []
+    for q in range(half):
+        cpart[q, 0:3 * band, :] = cpart[q, 0:3 * band, :] + cown[core, q, 0:3 * band, :]
+    for off in range(1, half):
+        copy = pltpu.make_async_remote_copy(
+            src_ref=cpart.at[lax.rem(me // 2 + off, half)], dst_ref=crecv.at[off - 1],
+            send_sem=csem.at[off - 1], recv_sem=crsem.at[off - 1],
+            device_id=peer(off), device_id_type=MESH)
+        copy.start()
+        ccopies.append(copy)
+    along(1, z, True, True, always)
+    along(2, z, True, True, always)
 
     low = pltpu.make_async_remote_copy(
-        src_ref=planes.at[:, band - 1], dst_ref=xpad.at[:, 0], send_sem=hsend.at[0], recv_sem=hrecv.at[0],
+        src_ref=xpad.at[:, band], dst_ref=xpad.at[:, 0], send_sem=hsend.at[0], recv_sem=hrecv.at[0],
         device_id=(g, lax.rem(me + 1, n)), device_id_type=MESH)
     high = pltpu.make_async_remote_copy(
-        src_ref=planes.at[:, 0], dst_ref=xpad.at[:, band + 1], send_sem=hsend.at[1], recv_sem=hrecv.at[1],
+        src_ref=xpad.at[:, 1], dst_ref=xpad.at[:, band + 1], send_sem=hsend.at[1], recv_sem=hrecv.at[1],
         device_id=(g, lax.rem(me + n - 1, n)), device_id_type=MESH)
     pl.when(me < n - 1)(low.start)
     pl.when(me > 0)(high.start)
 
-    for p in range(3):
-        total = planes[p, 0].astype(jnp.float32)
-        for i in range(1, band):
-            total = total + planes[p, i].astype(jnp.float32)
-        for d in range(n):
-            cown[d, p * band:(p + 1) * band, :] = total[d * band:(d + 1) * band, :]
-    ccopies = []
-    for off in range(1, n):
-        peer = lax.rem(me + off, n)
-        copy = pltpu.make_async_remote_copy(
-            src_ref=cown.at[peer], dst_ref=crecv.at[off - 1], send_sem=csem.at[off - 1],
-            recv_sem=crsem.at[off - 1], device_id=(g, peer), device_id_type=MESH)
-        copy.start()
-        ccopies.append(copy)
     lsend[...] = jnp.zeros(lsend.shape, lsend.dtype)
-    rows = []
     for p in range(3):
         for i in range(band):
-            rows.append(jnp.sum(planes[p, i].astype(jnp.float32), axis=0, keepdims=True) / width)
-    for index, row in enumerate(rows):
-        lsend[PAD + index:PAD + index + 1, :] = row
+            row = jnp.sum(xpad[p, 1 + i].astype(jnp.float32), axis=0, keepdims=True) / width
+            lsend[PAD + p * band + i:PAD + p * band + i + 1, :] = row
 
     def step(d):
         for k in range(3):
@@ -139,7 +156,9 @@
                 @pl.when(valid)
                 def _():
                     landed(k, s)
-                along(k, zz, up, down, valid)
+                if split and d == nz - 1:
+                    start(valid & (lax.rem(core + g, 2) == 0), k, s, twin)
+                along(k, zz, up, down, valid, d == nz - 2)
             for zz, valid in spread(d - 1):
                 sideways(k, zz, valid)
             if split and d >= 2:
@@ -151,25 +170,39 @@
             return [(z, always)]
         return [(z - d, z - d >= 0), (z + d, z + d < nz)]
 
-    step(1)
-
     for copy in ccopies:
         copy.wait_recv()
-    total = cown[me][0:3 * band]
-    for off in range(1, n):
+    total = cpart[me // 2, 0:3 * band, :]
+    for off in range(1, half):
         total = total + crecv[off - 1, 0:3 * band, :]
     lsend[0:3 * band, :] = total / width
     lines[me] = lsend[...].astype(jnp.bfloat16)
     lcopies = []
-    for off in range(1, n):
-        peer = lax.rem(me + off, n)
+
+    def send_line(src, sem, device):
         copy = pltpu.make_async_remote_copy(
-            src_ref=lines.at[me], dst_ref=lines.at[me], send_sem=lsem.at[off - 1],
-            recv_sem=lrsem.at[me], device_id=(g, peer), device_id_type=MESH)
+            src_ref=lines.at[src], dst_ref=lines.at[src], send_sem=sem, recv_sem=lrsem.at[src],
+            device_id=device, device_id_type=MESH)
         copy.start()
         lcopies.append(copy)
 
-    for d in range(2, nz):
+    def line_landed(src):
+        pltpu.make_async_remote_copy(
+            src_ref=lines.at[src], dst_ref=lines.at[src], send_sem=lsem.at[0], recv_sem=lrsem.at[src],
+            device_id=partner, device_id_type=MESH).wait_recv()
+
+    for off in range(1, half):
+        send_line(me, lsem.at[off], peer(off))
+    send_line(me, lsem.at[0], partner)
+
+    step(1)
+    if nz > 2:
+        step(2)
+    for off in range(1, half):
+        src = lax.rem(me + 2 * off, n)
+        line_landed(src)
+        send_line(src, fsem.at[off - 1], partner)
+    for d in range(3, nz):
         step(d)
     for k in range(3):
         for zz, valid in spread(nz - 1):
@@ -203,11 +236,8 @@
                 acc = part if acc is None else acc + part
             ybuf[b, p] = acc.reshape(band, width, chans)
 
-    for off in range(1, n):
-        src = lax.rem(me + off, n)
-        pltpu.make_async_remote_copy(
-            src_ref=lines.at[src], dst_ref=lines.at[src], send_sem=lsem.at[0], recv_sem=lrsem.at[src],
-            device_id=partner, device_id_type=MESH).wait_recv()
+    for q in range(half):
+        line_landed(2 * q + 1 - core)
     vrows = (PAD + 2 * band, 2 * band, band)
     for s in range(n):
         block = lines[s].astype(jnp.float32)
@@ -257,6 +287,7 @@
         pl.when(cond)(copy.wait_send)
     pl.when(me < n - 1)(low.wait_send)
     pl.when(me > 0)(high.wait_send)
+    swap.wait_send()
     for copy in ccopies + lcopies:
         copy.wait_send()
 
@@ -270,23 +301,24 @@
     return pl.pallas_call(
         functools.partial(fused, n, split),
         out_shape=jax.ShapeDtypeStruct(planes.shape, planes.dtype),
-        in_specs=[vmem, vmem],
+        in_specs=[pl.BlockSpec(memory_space=pltpu.HBM)] * 2,
         out_specs=vmem,
         scratch_shapes=[
             pltpu.VMEM((27, chans, chans), jnp.bfloat16),
             pltpu.VMEM((3, band + 2, width, chans), jnp.bfloat16),
-            pltpu.VMEM((n, PAD, chans), jnp.float32),
-            pltpu.VMEM((n - 1, PAD, chans), jnp.float32),
+            pltpu.VMEM((2, n // 2, PAD, chans), jnp.float32),
+            pltpu.VMEM((n // 2, PAD, chans), jnp.float32),
+            pltpu.VMEM((n // 2 - 1, PAD, chans), jnp.float32),
             pltpu.VMEM((2 * PAD, chans), jnp.float32),
             pltpu.VMEM((n, 2 * PAD, chans), jnp.bfloat16),
             pltpu.VMEM((3 * width, chans), jnp.float32),
             pltpu.VMEM((3 * depth, chans), jnp.float32),
             pltpu.VMEM((3, 3, band, width, chans), jnp.float32),
-            dma((160,)), dma((3, n)), dma((2,)), dma((2,)),
-            dma((n - 1,)), dma((n - 1,)), dma((n - 1,)), dma((n,)),
+            dma((192,)), dma((3, n)), dma((2,)), dma((2,)), dma((2,)),
+            dma((n // 2 - 1,)), dma((n // 2 - 1,)), dma((n // 2,)), dma((n,)), dma((n // 2 - 1,)), dma((2,)),
         ],
         compiler_params=pltpu.CompilerParams(
-            collective_id=0, has_side_effects=True, vmem_limit_bytes=40 * 1024 * 1024),
+            collective_id=0, has_side_effects=True, vmem_limit_bytes=60 * 1024 * 1024),
     )(planes, conv_weight.reshape(27, count, chans))
 
 
@@ -352,7 +384,7 @@
 
     def local(planes, conv_weight):
         band, width, chans = planes.shape[1:]
-        fits = n % 4 == 0 and 3 * band <= PAD and width % 16 == 0 and conv_weight.shape[3] % 16 == 0
+        fits = n % 8 == 0 and n > 8 and 3 * band <= PAD and width % 16 == 0 and conv_weight.shape[3] % 16 == 0
         if fits and band * n == width:
             return banded(n, split, planes, conv_weight)
         return body(planes, conv_weight)

time: 45.5 us -> 45.2 us (level)
  local copies, waits for them, and re-layouts: 2.56 us -> 1.64 us
    unnamed x5 -> x1, local copies, waits for them, and re-layouts: 2.56 us -> 1.64 us
where the time goes in v2:
time: 45.2 us; the launch traced here: 44.6 us
  Pallas kernels  43 us (95%)
  local copies, waits for them, and re-layouts  1.64 us (4%)
    pallas_call x1, Pallas kernels, banded(): pl.pallas_call(functools.partial(fused, n, split), out_shape=jax.ShapeDty...  43 us
    unnamed x1, local copies, waits for them, and re-layouts  1.64 us

profile of v2, /device:TPU:0, one launch (start us, length us, event | category | flops | bytes accessed | tf_op | source)
XLA Modules:
  0.0 44.6 jit_solution(14372241866451268484)
XLA Ops:
  0.0 43.0 %shard_map.28 = bf16[3,3,48,256]{3,2,1,0:T(8,128)(2,1)} custom-call(bf16[3,3,48,256]{3,2,1,0:T(8,128)(2,1)} %planes.1, bf16[27,16,256]{2,1,0:T(8,128)(2,1)} %bitcast.1), custom_call_target="tpu_custom_call" | custom-call | tf_op jit(solution)/shard_map/pallas_call | solution.py:301
  43.0 1.6 %copy.4 = bf16[3,3,48,256]{3,2,1,0:T(8,128)(2,1)} copy(bf16[3,3,48,256]{3,2,1,0:T(8,128)(2,1)} %shard_map.28) | data formatting | bytes 442368

commit v3 on v2

--- a/solution.py
+++ b/solution.py
@@ -9,6 +9,8 @@
 
 MESH = pl.DeviceIdType.MESH
 PAD = 16
+PIECES = 3
+TAPS = 27 // PIECES
 
 
 def fused(n, split, planes, w, out, wbuf, xpad, cown, cpart, crecv, lsend, lines, vbuf, ubuf, ybuf,
@@ -71,7 +73,7 @@
     sends = []
 
     def start(cond, k, s, dev):
-        region = wbuf.at[pl.ds(9 * k, 9), pl.ds(pl.multiple_of(s * count, count), count), :]
+        region = wbuf.at[pl.ds(TAPS * k, TAPS), pl.ds(pl.multiple_of(s * count, count), count), :]
         copy = pltpu.make_async_remote_copy(
             src_ref=region, dst_ref=region, send_sem=wsend.at[len(sends)], recv_sem=wrecv.at[k, s],
             device_id=dev, device_id_type=MESH)
@@ -79,7 +81,7 @@
         sends.append((cond, copy))
 
     def landed(k, s):
-        region = wbuf.at[pl.ds(9 * k, 9), pl.ds(pl.multiple_of(s * count, count), count), :]
+        region = wbuf.at[pl.ds(TAPS * k, TAPS), pl.ds(pl.multiple_of(s * count, count), count), :]
         pltpu.make_async_remote_copy(
             src_ref=region, dst_ref=region, send_sem=wsend.at[0], recv_sem=wrecv.at[k, s],
             device_id=partner, device_id_type=MESH).wait_recv()
@@ -130,8 +132,8 @@
             device_id=peer(off), device_id_type=MESH)
         copy.start()
         ccopies.append(copy)
-    along(1, z, True, True, always)
-    along(2, z, True, True, always)
+    for k in range(1, PIECES):
+        along(k, z, True, True, always)
 
     low = pltpu.make_async_remote_copy(
         src_ref=xpad.at[:, band], dst_ref=xpad.at[:, 0], send_sem=hsend.at[0], recv_sem=hrecv.at[0],
@@ -149,7 +151,7 @@
             lsend[PAD + p * band + i:PAD + p * band + i + 1, :] = row
 
     def step(d):
-        for k in range(3):
+        for k in range(PIECES):
             for zz, up, down, valid in ((z - d, True, False, z - d >= 0), (z + d, False, True, z + d < nz)):
                 s = rank(zz, y, core)
 
@@ -204,12 +206,12 @@
         send_line(src, fsem.at[off - 1], partner)
     for d in range(3, nz):
         step(d)
-    for k in range(3):
+    for k in range(PIECES):
         for zz, valid in spread(nz - 1):
             sideways(k, zz, valid)
     if split:
         for d in (nz - 2, nz - 1):
-            for k in range(3):
+            for k in range(PIECES):
                 for zz, valid in spread(d):
                     third(k, zz, valid)
 
@@ -221,7 +223,11 @@
     def _():
         high.wait_recv()
 
-    def gathered(k):
+    def gathered(block):
+        for k in range(block * PIECES // 3, (block + 1) * PIECES // 3):
+            collected(k)
+
+    def collected(k):
         for zz in range(nz):
             for yy in range(2):
                 landed(k, rank(zz, yy, 1 - core))
@@ -314,7 +320,7 @@
             pltpu.VMEM((3 * width, chans), jnp.float32),
             pltpu.VMEM((3 * depth, chans), jnp.float32),
             pltpu.VMEM((3, 3, band, width, chans), jnp.float32),
-            dma((192,)), dma((3, n)), dma((2,)), dma((2,)), dma((2,)),
+            dma((64 * PIECES,)), dma((PIECES, n)), dma((2,)), dma((2,)), dma((2,)),
             dma((n // 2 - 1,)), dma((n // 2 - 1,)), dma((n // 2,)), dma((n,)), dma((n // 2 - 1,)), dma((2,)),
         ],
         compiler_params=pltpu.CompilerParams(
@@ -380,7 +386,7 @@
 
 def solution(mesh):
     n = mesh.shape["rows"]
-    split = mesh.shape["groups"] == 2
+    split = False
 
     def local(planes, conv_weight):
         band, width, chans = planes.shape[1:]

time: 45.2 us -> 36.9 us (0.82)
  Pallas kernels: 43 us -> 35.1 us
    pallas_call x1, Pallas kernels: 43 us -> 35.1 us  [banded(): pl.pallas_call(functools.partial(fused, n, split), out_shape=jax.ShapeDty...]
where the time goes in v3:
time: 36.9 us; the launch traced here: 36.8 us
  Pallas kernels  35.1 us (95%)
  local copies, waits for them, and re-layouts  1.64 us (4%)
    pallas_call x1, Pallas kernels, banded(): pl.pallas_call(functools.partial(fused, n, split), out_shape=jax.ShapeDty...  35.1 us
    unnamed x1, local copies, waits for them, and re-layouts  1.64 us

profile of v3, /device:TPU:0, one launch (start us, length us, event | category | flops | bytes accessed | tf_op | source)
XLA Modules:
  0.0 36.8 jit_solution(9057340948758598253)
XLA Ops:
  0.0 35.1 %shard_map.28 = bf16[3,3,48,256]{3,2,1,0:T(8,128)(2,1)} custom-call(bf16[3,3,48,256]{3,2,1,0:T(8,128)(2,1)} %planes.1, bf16[27,16,256]{2,1,0:T(8,128)(2,1)} %bitcast.1), custom_call_target="tpu_custom_call" | custom-call | tf_op jit(solution)/shard_map/pallas_call | solution.py:307
  35.1 1.6 %copy.4 = bf16[3,3,48,256]{3,2,1,0:T(8,128)(2,1)} copy(bf16[3,3,48,256]{3,2,1,0:T(8,128)(2,1)} %shard_map.28) | data formatting | bytes 442368
